TPU v7x, 512 devices: a whole 4x4x16 slice. The times are simulated.
512 devices in a mesh: slab: 32 (over z, core), row: 4 (over y), col: 4 (over x).
Axes of the slice: x: 4, y: 4, z: 16, core: 2. Of those that a mesh axis runs over, the one named last changes fastest.
Arguments:
- coupling: float32 [512, 512], replicated, may hold values from -1 to 1, as said below
- disorder: int32 [64, 512], P('slab'), may hold values from 0 to 1023
- gain_level: int32 [64, 512], P('slab'), may hold values from 0 to 3, as said below
Outputs:
- reduced: float32 [32, 2, 512, 512], P('slab', None, ('row', 'col'))
- coupled: float32 [32, 2, 512, 512], P('slab', None, ('row', 'col'))
Inputs may be any that keep to these rules, and one draw needn't show every extreme that they name: symmetric: coupling[p, q] = coupling[q, p]. `gain_level`: in each slice the nonzero entries fill one run of 256 consecutive points and lie in 1 to 3; all other entries are 0.
All inputs are finite; a program needn't handle non-finite values.
Results may differ from a plain program's by a relative error of at most 0.00014.
Values sent between devices are 32-bit elements; how exact they have to be, the bound alone decides.
A program may use at most 64 MiB of HBM per device.

v0:
```python
import jax
import jax.numpy as jnp
from jax import lax
from jax.experimental import pallas as pl
from jax.experimental.pallas import tpu as pltpu
from jax.sharding import PartitionSpec as P

DEGREE = 8
MESH = pl.DeviceIdType.MESH
F32 = jnp.float32
BF16 = jnp.bfloat16

energy_level = 0.5
absorption = 2.0
disorder_width = 2.0
gain_step = 0.25
hop_square = 2.25

N = 512
B = 32
T = 128
H = 256
LOW, HIGH, ALL = slice(0, H), slice(H, N), slice(0, N)


def dot(a, b):
    return jnp.dot(a, b, preferred_element_type=F32)


def split(a):
    hi = a.astype(BF16)
    return hi, (a - hi.astype(F32)).astype(BF16)


def product(hi, lo, weight_hi, weight_lo):
    return (dot(hi, weight_hi) + dot(lo, weight_hi)) + dot(hi, weight_lo)


def times(a_re, a_im, b_re, b_im):
    return a_re * b_re - a_im * b_im, a_re * b_im + a_im * b_re


def kernel(coupling_hbm, disorder_hbm, gain_hbm, reduced_ref, coupled_ref,
           kf, kh, kl, levels, a_buf, a_cols, w, q, qh, ql, m, mh, ml, lh, ll,
           acc, base, lband, x_send, z_send, y_send, x_recv, z_recv, y_recv,
           load_sem, a_sems, x_sems, z_sems, y_sems):
    slab = lax.axis_index("slab")
    band = (lax.axis_index("row") * lax.axis_size("col") + lax.axis_index("col")) * B
    slabs = lax.axis_size("slab")
    has_behind, has_ahead = slab > 0, slab < slabs - 1
    ahead, behind = jnp.minimum(slab + 1, slabs - 1), jnp.maximum(slab - 1, 0)

    loads = [pltpu.make_async_copy(source, target, load_sem.at[number]) for number, (source, target) in enumerate(
        ((disorder_hbm, levels.at[0]), (gain_hbm, levels.at[1]), (coupling_hbm, kf)))]
    for load in loads:
        load.start()

    barrier = pltpu.get_barrier_semaphore()

    @pl.when(has_ahead)
    def _():
        pl.semaphore_signal(barrier, inc=1, device_id={"slab": ahead}, device_id_type=MESH)

    @pl.when(has_behind)
    def _():
        pl.semaphore_signal(barrier, inc=1, device_id={"slab": behind}, device_id_type=MESH)

    def remote(source, target, sems, device):
        return pltpu.make_async_remote_copy(
            src_ref=source, dst_ref=target, send_sem=sems.at[0], recv_sem=sems.at[1],
            device_id={"slab": device}, device_id_type=MESH)

    a_copy = remote(a_buf.at[1], a_buf.at[0], a_sems, ahead)
    x_copy = remote(x_send, x_recv, x_sems, behind)
    z_copy = remote(z_send, z_recv, z_sems, behind)
    y_copy = remote(y_send, y_recv, y_sems, ahead)

    eye = lax.broadcasted_iota(jnp.int32, (T, T), 0) == lax.broadcasted_iota(jnp.int32, (T, T), 1)

    def diagonal_of(ref):
        return jnp.concatenate(
            [jnp.sum(jnp.where(eye, ref[t * T:(t + 1) * T, t * T:(t + 1) * T], 0.0), axis=0, keepdims=True)
             for t in range(N // T)], axis=1)

    loads[0].wait()
    loads[1].wait()
    potential = disorder_width * (levels[0].astype(F32) / 1023.0 - 0.5)
    gain = gain_step * levels[1].astype(F32)
    loads[2].wait()
    k_diag = diagonal_of(kf)
    d_re = (energy_level - potential) - k_diag
    d_im = absorption - gain
    size = d_re[1:2] * d_re[1:2] + d_im[1:2] * d_im[1:2]
    a_buf[1, 0:1, :] = d_re[1:2] / size
    a_buf[1, 1:2, :] = -d_im[1:2] / size

    for t in range(N // T):
        rows = slice(t * T, (t + 1) * T)
        ids = lax.broadcasted_iota(jnp.int32, (T, N), 0) + t * T
        off = jnp.where(ids == lax.broadcasted_iota(jnp.int32, (T, N), 1), 0.0, kf[rows, :])
        kf[rows, :] = off
        hi, lo = split(off)
        kh[rows, :] = hi
        kl[rows, :] = lo

    def mirror(ref, part):
        ref[part, LOW, HIGH] = ref[part, HIGH, LOW].T

    def whole_m(which, a_re, a_im, after_first):
        for t in range(N // T):
            cols = slice(t * T, (t + 1) * T)
            a_cols[0, cols, :] = jnp.broadcast_to(a_re[:, cols], (T, T)).T
            a_cols[1, cols, :] = jnp.broadcast_to(a_im[:, cols], (T, T)).T

        def scaled(rows):
            re, im = times(w[0, rows, :], w[1, rows, :], a_re, a_im)
            return split(jnp.concatenate([re, im], axis=0))

        for step in range(3):
            for rows, cols in ((LOW, LOW), (HIGH, ALL)):
                if step == 0:
                    hi, lo = split(jnp.concatenate([kf[rows, :] * a_re, kf[rows, :] * a_im], axis=0))
                else:
                    hi, lo = scaled(rows)
                t = product(hi, lo, kh[:, cols], kl[:, cols])
                w[0, rows, cols] = t[:H]
                w[1, rows, cols] = t[H:]
                if step == 0:
                    q[0, rows, cols] = kf[rows, cols] + t[:H]
                    q[1, rows, cols] = t[H:]
                elif step == 1:
                    q[0, rows, cols] = q[0, rows, cols] + t[:H]
                    q[1, rows, cols] = q[1, rows, cols] + t[H:]
                else:
                    q[0, rows, cols] = q[0, rows, cols] + t[:H]
                    q[1, rows, cols] = q[1, rows, cols] + t[H:]
            for part in range(2):
                mirror(w, part)
            if step == 0:
                after_first()
        for part in range(2):
            mirror(q, part)
            hi, lo = split(q[part])
            qh[part] = hi
            ql[part] = lo
        for rows, cols in ((LOW, LOW), (HIGH, ALL)):
            hi, lo = scaled(rows)
            t = product(hi, lo, qh[0, :, cols], ql[0, :, cols])
            u = product(hi, lo, qh[1, :, cols], ql[1, :, cols])
            n_re = q[0, rows, cols] + (t[:H] - u[H:])
            n_im = q[1, rows, cols] + (t[H:] + u[:H])
            n_re, n_im = times(n_re, n_im, a_re[:, cols], a_im[:, cols])
            width = n_re.shape[1]
            diagonal = ((lax.broadcasted_iota(jnp.int32, (H, width), 0) + rows.start)
                        == (lax.broadcasted_iota(jnp.int32, (H, width), 1) + cols.start))
            n_re = n_re + jnp.where(diagonal, 1.0, 0.0)
            c_re = jnp.concatenate([a_cols[0, rows, :]] * (width // T), axis=1) * -hop_square
            c_im = jnp.concatenate([a_cols[1, rows, :]] * (width // T), axis=1) * -hop_square
            m_re, m_im = times(n_re, n_im, c_re, c_im)
            m[which, 0, rows, cols] = m_re
            m[which, 1, rows, cols] = m_im
        for part in range(2):
            mirror(m.at[which], part)
            hi, lo = split(m[which, part])
            mh[which, part] = hi
            ml[which, part] = lo

    def meet():
        pl.semaphore_wait(barrier, has_ahead.astype(jnp.int32) + has_behind.astype(jnp.int32))

        @pl.when(has_ahead)
        def _():
            a_copy.start()

    whole_m(1, a_buf[1, 0:1, :], a_buf[1, 1:2, :], meet)

    @pl.when(has_behind)
    def _():
        a_copy.wait_recv()

    whole_m(0, jnp.where(has_behind, a_buf[0, 0:1, :], 0.0), jnp.where(has_behind, a_buf[0, 1:2, :], 0.0), lambda: None)

    m_diag = [[diagonal_of(m.at[which, part]) for part in range(2)] for which in range(2)]
    d_re = (d_re[0:1] + m_diag[1][0]) + m_diag[0][0]
    d_im = (d_im[0:1] + m_diag[1][1]) + m_diag[0][1]
    size = d_re * d_re + d_im * d_im
    i_re = d_re / size
    i_im = -d_im / size
    for t in range(N // T):
        rows = slice(t * T, (t + 1) * T)
        off = (lax.broadcasted_iota(jnp.int32, (T, N), 0) + t * T) != lax.broadcasted_iota(jnp.int32, (T, N), 1)
        hi, lo = split(jnp.where(off, (m[1, 0, rows, :] - kf[rows, :]) + m[0, 0, rows, :], 0.0))
        lh[0, rows, :] = hi
        ll[0, rows, :] = lo
        hi, lo = split(jnp.where(off, m[1, 1, rows, :] + m[0, 1, rows, :], 0.0))
        lh[1, rows, :] = hi
        ll[1, rows, :] = lo
    mine = pl.ds(pl.multiple_of(band, B), B)
    unit = (lax.broadcasted_iota(jnp.int32, (B, N), 0) + band) == lax.broadcasted_iota(jnp.int32, (B, N), 1)
    lband[0] = jnp.where(unit, d_re, (m[1, 0, mine, :] - kf[mine, :]) + m[0, 0, mine, :])
    lband[1] = jnp.where(unit, d_im, m[1, 1, mine, :] + m[0, 1, mine, :])

    W2 = 2 * B
    for which in range(2):
        re, im = times(m[which, 0, mine, :], m[which, 1, mine, :], i_re, i_im)
        for ref in (base, acc):
            ref[which * B:(which + 1) * B, :] = re
            ref[W2 + which * B:W2 + (which + 1) * B, :] = im

    def by_complex(rows, hi_ref, lo_ref):
        hi, lo = split(rows)
        half = rows.shape[0] // 2
        both = jnp.concatenate([hi, lo], axis=0)
        t = dot(both, hi_ref[0])
        t = (t[:2 * half] + t[2 * half:]) + dot(hi, lo_ref[0])
        u = dot(both, hi_ref[1])
        u = (u[:2 * half] + u[2 * half:]) + dot(hi, lo_ref[1])
        return t[:half] - u[half:], t[half:] + u[:half]

    def inverse_step(index, carry):
        re, im = times(*by_complex(acc[...], lh, ll), i_re, i_im)
        acc[:W2, :] = base[:W2, :] - re
        acc[W2:, :] = base[W2:, :] - im
        return carry
    lax.fori_loop(0, DEGREE, inverse_step, 0)

    terms = by_complex(acc[...], mh.at[1], ml.at[1])
    for part in range(2):
        z_send[part] = -terms[part][:B]
        y_send[part] = terms[part][B:]

    @pl.when(has_behind)
    def _():
        z_copy.start()

    @pl.when(has_ahead)
    def _():
        y_copy.start()
    first = jnp.concatenate([acc[0:B, :], acc[W2:W2 + B, :]], axis=0)
    terms = by_complex(first, mh.at[0], ml.at[0])
    for part in range(2):
        x_send[part] = terms[part]

    @pl.when(has_behind)
    def _():
        x_copy.start()
        y_copy.wait_recv()

    @pl.when(has_ahead)
    def _():
        z_copy.wait_recv()
        x_copy.wait_recv()
    reduced_ref[...] = (lband[...] - jnp.where(has_ahead, x_recv[...], 0.0)) - jnp.where(has_behind, y_recv[...], 0.0)
    coupled_ref[...] = jnp.where(has_ahead, z_recv[...], 0.0)

    @pl.when(has_behind)
    def _():
        z_copy.wait_send()
        x_copy.wait_send()

    @pl.when(has_ahead)
    def _():
        a_copy.wait_send()
        y_copy.wait_send()


def local(coupling, disorder, gain_level):
    vmem = pl.BlockSpec(memory_space=pltpu.VMEM)
    hbm = pl.BlockSpec(memory_space=pl.ANY)
    square = (N, N)
    band = pltpu.VMEM((2, B, N), F32)
    pair = pltpu.SemaphoreType.DMA((2,))
    scratch = [
        pltpu.VMEM(square, F32),
        pltpu.VMEM(square, BF16),
        pltpu.VMEM(square, BF16),
        pltpu.VMEM((2, 2, N), jnp.int32),
        pltpu.VMEM((2, 8, N), F32),
        pltpu.VMEM((2, N, T), F32),
        pltpu.VMEM((2,) + square, F32),
        pltpu.VMEM((2,) + square, F32),
        pltpu.VMEM((2,) + square, BF16),
        pltpu.VMEM((2,) + square, BF16),
        pltpu.VMEM((2, 2) + square, F32),
        pltpu.VMEM((2, 2) + square, BF16),
        pltpu.VMEM((2, 2) + square, BF16),
        pltpu.VMEM((2,) + square, BF16),
        pltpu.VMEM((2,) + square, BF16),
        pltpu.VMEM((4 * B, N), F32),
        pltpu.VMEM((4 * B, N), F32),
        band, band, band, band, band, band, band,
        pltpu.SemaphoreType.DMA((3,)),
        pair, pair, pair, pair,
    ]
    reduced, coupled = pl.pallas_call(
        kernel,
        out_shape=[jax.ShapeDtypeStruct((2, B, N), F32)] * 2,
        in_specs=[hbm, hbm, hbm],
        out_specs=[vmem, vmem],
        scratch_shapes=scratch,
        compiler_params=pltpu.CompilerParams(
            collective_id=0, has_side_effects=True, vmem_limit_bytes=32 * 2**20),
        cost_estimate=pl.CostEstimate(flops=16 * 10**9, bytes_accessed=2 * 2**20, transcendentals=0),
        name="reduce_two_levels",
    )(coupling, disorder, gain_level)
    return reduced[None], coupled[None]


def solution(mesh):
    return jax.shard_map(
        local,
        mesh=mesh,
        in_specs=(P(), P("slab", None), P("slab", None)),
        out_specs=(P("slab", None, ("row", "col"), None), P("slab", None, ("row", "col"), None)),
        check_vma=False,
    )
```

profile of v0, /device:TPU:1, one launch (start us, length us, event | category | flops | bytes accessed | tf_op | source)
XLA Modules:
  0.0 37.8 jit_solution(4920910152863008202)
XLA Ops:
  0.6 0.0 copy-start
  0.6 1.2 %copy-done = f32[512,512]{1,0:T(8,128)S(1)} copy-done((f32[512,512]{1,0:T(8,128)S(1)}, f32[512,512]{1,0:T(8,128)}, u32[]{:S(2)}) %copy-start) | copy-done | bytes 1048600
  1.9 0.0 copy-start.1
  1.9 0.7 %copy-done.1 = s32[2,512]{1,0:T(2,128)S(1)} copy-done((s32[2,512]{1,0:T(2,128)S(1)}, s32[2,512]{1,0:T(2,128)}, u32[]{:S(2)}) %copy-start.1) | copy-done | bytes 4120
  2.5 0.0 copy-start.2
  2.5 0.7 %copy-done.2 = s32[2,512]{1,0:T(2,128)S(1)} copy-done((s32[2,512]{1,0:T(2,128)S(1)}, s32[2,512]{1,0:T(2,128)}, u32[]{:S(2)}) %copy-start.2) | copy-done | bytes 4120
  3.2 33.2 %reduce_two_levels.1 = (f32[2,32,512]{2,1,0:T(8,128)S(1)}, f32[2,32,512]{2,1,0:T(8,128)S(1)}) custom-call(f32[512,512]{1,0:T(8,128)S(1)} %copy-done, s32[2,512]{1,0:T(2,128)S(1)} %copy-done.1, s32[2,512]{1,0:T(2,128)S(1)} %copy-done.2), custom_call_target="tpu_custom_call" | custom-call | flops 16000000000 | bytes 2097152 | tf_op jit(solution)/shard_map/reduce_two_levels/pallas_call | solution.py:295
  36.5 0.7 %copy.7 = f32[1,2,32,512]{3,2,1,0:T(8,128)} copy(f32[1,2,32,512]{3,2,1,0:T(8,128)S(1)} %bitcast.3) | data formatting | bytes 262144
  37.1 0.7 %copy.8 = f32[1,2,32,512]{3,2,1,0:T(8,128)} copy(f32[1,2,32,512]{3,2,1,0:T(8,128)S(1)} %bitcast.2) | data formatting | bytes 262144
Async XLA Ops:
  0.6 1.2 %copy-start = (f32[512,512]{1,0:T(8,128)S(1)}, f32[512,512]{1,0:T(8,128)}, u32[]{:S(2)}) copy-start(f32[512,512]{1,0:T(8,128)} %coupling_hbm.1) | copy-start | bytes 3145732
  1.9 0.7 %copy-start.1 = (s32[2,512]{1,0:T(2,128)S(1)}, s32[2,512]{1,0:T(2,128)}, u32[]{:S(2)}) copy-start(s32[2,512]{1,0:T(2,128)} %disorder_hbm.1) | copy-start | bytes 12292
  2.5 0.7 %copy-start.2 = (s32[2,512]{1,0:T(2,128)S(1)}, s32[2,512]{1,0:T(2,128)}, u32[]{:S(2)}) copy-start(s32[2,512]{1,0:T(2,128)} %gain_hbm.1) | copy-start | bytes 12292
where the time goes:
time: 38 us; the launch traced here: 37.8 us
  Pallas kernels  33.2 us (87%)
  local copies, waits for them, and re-layouts  3.9 us (10%)
  between operations  0.65 us (2%)
    pallas_call x1, Pallas kernels, local(): pl.pallas_call(kernel, out_shape=[jax.ShapeDtypeStruct((2, B, N), F32)] *...  33.2 us
    unnamed x8, local copies, waits for them, and re-layouts  3.9 us

commit v1 on v0

v1 whole, which is shorter than its diff:
```python
import jax
import jax.numpy as jnp
from jax import lax
from jax.experimental import pallas as pl
from jax.experimental.pallas import tpu as pltpu
from jax.sharding import PartitionSpec as P

DEGREE = 8
MESH = pl.DeviceIdType.MESH
F32 = jnp.float32
BF16 = jnp.bfloat16

energy_level = 0.5
absorption = 2.0
disorder_width = 2.0
gain_step = 0.25
hop_square = 2.25

N = 512
B = 32
T = 128
H = 256
LOW, HIGH, ALL = slice(0, H), slice(H, N), slice(0, N)


def dot(a, b):
    return jnp.dot(a, b, preferred_element_type=F32)


def split(a):
    hi = a.astype(BF16)
    return hi, (a - hi.astype(F32)).astype(BF16)


def product(hi, lo, weight_hi, weight_lo):
    return (dot(hi, weight_hi) + dot(lo, weight_hi)) + dot(hi, weight_lo)


def times(a_re, a_im, b_re, b_im):
    return a_re * b_re - a_im * b_im, a_re * b_im + a_im * b_re


def kernel(coupling_ref, potential_ref, gain_ref, kept_ref, y_ref, minus_z_ref,
           kf, kh, kl, a_buf, a_cols, w, q, qh, ql, m, mh, ml, lh, ll,
           acc, base, lband, f_send, z_send, s_send, f_recv, z_recv, s_recv,
           a_sems, f_sems, z_sems, s_sems):
    slab = lax.axis_index("slab")
    band = (lax.axis_index("row") * lax.axis_size("col") + lax.axis_index("col")) * B
    slabs = lax.axis_size("slab")
    has_behind, has_ahead = slab > 0, slab < slabs - 1
    ahead, behind = jnp.minimum(slab + 1, slabs - 1), jnp.maximum(slab - 1, 0)

    barrier = pltpu.get_barrier_semaphore()

    @pl.when(has_ahead)
    def _():
        pl.semaphore_signal(barrier, inc=1, device_id={"slab": ahead}, device_id_type=MESH)

    @pl.when(has_behind)
    def _():
        pl.semaphore_signal(barrier, inc=1, device_id={"slab": behind}, device_id_type=MESH)

    def remote(source, target, sems, device):
        return pltpu.make_async_remote_copy(
            src_ref=source, dst_ref=target, send_sem=sems.at[0], recv_sem=sems.at[1],
            device_id={"slab": device}, device_id_type=MESH)

    a_copy = remote(a_buf.at[1], a_buf.at[0], a_sems, ahead)
    f_copy = remote(f_send, f_recv, f_sems, behind)
    z_copy = remote(z_send, z_recv, z_sems, behind)
    s_copy = remote(s_send, s_recv, s_sems, ahead)

    eye = lax.broadcasted_iota(jnp.int32, (T, T), 0) == lax.broadcasted_iota(jnp.int32, (T, T), 1)

    def diagonal_of(ref):
        return jnp.concatenate(
            [jnp.sum(jnp.where(eye, ref[t * T:(t + 1) * T, t * T:(t + 1) * T], 0.0), axis=0, keepdims=True)
             for t in range(N // T)], axis=1)

    potential = potential_ref[...]
    gain = gain_ref[...]
    k_diag = diagonal_of(coupling_ref)
    d_re = (energy_level - potential) - k_diag
    d_im = absorption - gain
    size = d_re[1:2] * d_re[1:2] + d_im[1:2] * d_im[1:2]
    a_buf[1, 0:1, :] = d_re[1:2] / size
    a_buf[1, 1:2, :] = -d_im[1:2] / size

    for t in range(N // T):
        rows = slice(t * T, (t + 1) * T)
        ids = lax.broadcasted_iota(jnp.int32, (T, N), 0) + t * T
        off = jnp.where(ids == lax.broadcasted_iota(jnp.int32, (T, N), 1), 0.0, coupling_ref[rows, :])
        kf[rows, :] = off
        hi, lo = split(off)
        kh[rows, :] = hi
        kl[rows, :] = lo

    def whole_m(which, a_re, a_im, after_first):
        for t in range(N // T):
            cols = slice(t * T, (t + 1) * T)
            a_cols[0, cols, :] = jnp.broadcast_to(a_re[:, cols], (T, T)).T
            a_cols[1, cols, :] = jnp.broadcast_to(a_im[:, cols], (T, T)).T

        blocks = [(slice(r, r + T), ALL if r >= H else LOW) for r in (2 * T, 3 * T, 0, T)]

        def scaled(step, rows):
            if step == 0:
                re, im = kf[rows, :] * a_re, kf[rows, :] * a_im
            else:
                re, im = times(w[step - 1, 0, rows, :], w[step - 1, 1, rows, :], a_re, a_im)
            return re, im

        def mirror(ref, rows):
            if rows.start >= H:
                for part in range(2):
                    ref[part, LOW, rows] = ref[part, rows, LOW].T

        for step in range(3):
            for rows, cols in blocks:
                hi, lo = split(jnp.concatenate(scaled(step, rows), axis=0))
                t = product(hi, lo, kh[:, cols], kl[:, cols])
                w[step, 0, rows, cols] = t[:T]
                w[step, 1, rows, cols] = t[T:]
                mirror(w.at[step], rows)
            if step == 0:
                after_first()
        for part in range(2):
            for rows in (HIGH, LOW):
                total = (w[0, part, rows, :] + w[1, part, rows, :]) + w[2, part, rows, :]
                if part == 0:
                    total = total + kf[rows, :]
                q[part, rows, :] = total
                hi, lo = split(total)
                qh[part, rows, :] = hi
                ql[part, rows, :] = lo
        for rows in (HIGH, LOW):
            hi, lo = split(q[0, rows, :] + q[1, rows, :])
            qh[2, rows, :] = hi
            ql[2, rows, :] = lo
        for rows, cols in blocks:
            re, im = scaled(3, rows)
            both_re = product(*split(re), qh[0, :, cols], ql[0, :, cols])
            both_im = product(*split(im), qh[1, :, cols], ql[1, :, cols])
            crossed = product(*split(re + im), qh[2, :, cols], ql[2, :, cols])
            n_re = q[0, rows, cols] + (both_re - both_im)
            n_im = q[1, rows, cols] + ((crossed - both_re) - both_im)
            n_re, n_im = times(n_re, n_im, a_re[:, cols], a_im[:, cols])
            width = n_re.shape[1]
            diagonal = ((lax.broadcasted_iota(jnp.int32, (T, width), 0) + rows.start)
                        == (lax.broadcasted_iota(jnp.int32, (T, width), 1) + cols.start))
            n_re = n_re + jnp.where(diagonal, 1.0, 0.0)
            c_re = jnp.concatenate([a_cols[0, rows, :]] * (width // T), axis=1) * -hop_square
            c_im = jnp.concatenate([a_cols[1, rows, :]] * (width // T), axis=1) * -hop_square
            m_re, m_im = times(n_re, n_im, c_re, c_im)
            m[which, 0, rows, cols] = m_re
            m[which, 1, rows, cols] = m_im
            mirror(m.at[which], rows)
        for part in range(2):
            hi, lo = split(m[which, part])
            mh[which, part] = hi
            ml[which, part] = lo

    def meet():
        pl.semaphore_wait(barrier, has_ahead.astype(jnp.int32) + has_behind.astype(jnp.int32))

        @pl.when(has_ahead)
        def _():
            a_copy.start()

    whole_m(1, a_buf[1, 0:1, :], a_buf[1, 1:2, :], meet)

    @pl.when(has_behind)
    def _():
        a_copy.wait_recv()

    whole_m(0, jnp.where(has_behind, a_buf[0, 0:1, :], 0.0), jnp.where(has_behind, a_buf[0, 1:2, :], 0.0), lambda: None)

    m_diag = [[diagonal_of(m.at[which, part]) for part in range(2)] for which in range(2)]
    d_re = (d_re[0:1] + m_diag[1][0]) + m_diag[0][0]
    d_im = (d_im[0:1] + m_diag[1][1]) + m_diag[0][1]
    size = d_re * d_re + d_im * d_im
    i_re = d_re / size
    i_im = -d_im / size
    for t in range(N // T):
        rows = slice(t * T, (t + 1) * T)
        off = (lax.broadcasted_iota(jnp.int32, (T, N), 0) + t * T) != lax.broadcasted_iota(jnp.int32, (T, N), 1)
        hi, lo = split(jnp.where(off, (m[1, 0, rows, :] - kf[rows, :]) + m[0, 0, rows, :], 0.0))
        lh[0, rows, :] = hi
        ll[0, rows, :] = lo
        hi, lo = split(jnp.where(off, m[1, 1, rows, :] + m[0, 1, rows, :], 0.0))
        lh[1, rows, :] = hi
        ll[1, rows, :] = lo
    mine = pl.ds(pl.multiple_of(band, B), B)
    unit = (lax.broadcasted_iota(jnp.int32, (B, N), 0) + band) == lax.broadcasted_iota(jnp.int32, (B, N), 1)
    lband[0] = jnp.where(unit, d_re, (m[1, 0, mine, :] - kf[mine, :]) + m[0, 0, mine, :])
    lband[1] = jnp.where(unit, d_im, m[1, 1, mine, :] + m[0, 1, mine, :])

    W2 = 2 * B
    for which in range(2):
        re, im = times(m[which, 0, mine, :], m[which, 1, mine, :], i_re, i_im)
        for ref in (base, acc):
            ref[which * B:(which + 1) * B, :] = re
            ref[W2 + which * B:W2 + (which + 1) * B, :] = im

    def by_complex(rows, hi_ref, lo_ref):
        hi, lo = split(rows)
        half = rows.shape[0] // 2
        both = jnp.concatenate([hi, lo], axis=0)
        t = dot(both, hi_ref[0])
        t = (t[:2 * half] + t[2 * half:]) + dot(hi, lo_ref[0])
        u = dot(both, hi_ref[1])
        u = (u[:2 * half] + u[2 * half:]) + dot(hi, lo_ref[1])
        return t[:half] - u[half:], t[half:] + u[:half]

    def inverse_step(index, carry):
        re, im = times(*by_complex(acc[...], lh, ll), i_re, i_im)
        acc[:W2, :] = base[:W2, :] - re
        acc[W2:, :] = base[W2:, :] - im
        return carry
    lax.fori_loop(0, DEGREE, inverse_step, 0)

    for part in range(2):
        f_send[part * B:(part + 1) * B, :] = acc[part * W2:part * W2 + B, :]
        s_send[part * B:(part + 1) * B, :] = acc[part * W2 + B:(part + 1) * W2, :]

    @pl.when(has_behind)
    def _():
        f_copy.start()

    @pl.when(has_ahead)
    def _():
        s_copy.start()
    terms = by_complex(f_send[...], mh.at[1], ml.at[1])
    for part in range(2):
        z_send[part] = terms[part]

    @pl.when(has_behind)
    def _():
        z_copy.start()
        s_copy.wait_recv()
    terms = by_complex(jnp.where(has_behind, s_recv[...], 0.0), mh.at[0], ml.at[0])
    for part in range(2):
        y_ref[part] = terms[part]

    @pl.when(has_ahead)
    def _():
        f_copy.wait_recv()
    terms = by_complex(jnp.where(has_ahead, f_recv[...], 0.0), mh.at[1], ml.at[1])
    for part in range(2):
        kept_ref[part] = lband[part] - terms[part]

    @pl.when(has_ahead)
    def _():
        z_copy.wait_recv()
    minus_z_ref[...] = jnp.where(has_ahead, z_recv[...], 0.0)

    @pl.when(has_behind)
    def _():
        f_copy.wait_send()
        z_copy.wait_send()

    @pl.when(has_ahead)
    def _():
        a_copy.wait_send()
        s_copy.wait_send()


def local(coupling, disorder, gain_level):
    vmem = pl.BlockSpec(memory_space=pltpu.VMEM)
    square = (N, N)
    band = pltpu.VMEM((2, B, N), F32)
    rows = pltpu.VMEM((2 * B, N), F32)
    potential = disorder_width * (disorder.astype(F32) / 1023.0 - 0.5)
    gain = gain_step * gain_level.astype(F32)
    pair = pltpu.SemaphoreType.DMA((2,))
    scratch = [
        pltpu.VMEM(square, F32),
        pltpu.VMEM(square, BF16),
        pltpu.VMEM(square, BF16),
        pltpu.VMEM((2, 8, N), F32),
        pltpu.VMEM((2, N, T), F32),
        pltpu.VMEM((3, 2) + square, F32),
        pltpu.VMEM((2,) + square, F32),
        pltpu.VMEM((3,) + square, BF16),
        pltpu.VMEM((3,) + square, BF16),
        pltpu.VMEM((2, 2) + square, F32),
        pltpu.VMEM((2, 2) + square, BF16),
        pltpu.VMEM((2, 2) + square, BF16),
        pltpu.VMEM((2,) + square, BF16),
        pltpu.VMEM((2,) + square, BF16),
        pltpu.VMEM((4 * B, N), F32),
        pltpu.VMEM((4 * B, N), F32),
        band, rows, band, rows, rows, band, rows,
        pair, pair, pair, pair,
    ]
    kept, y, minus_z = pl.pallas_call(
        kernel,
        out_shape=[jax.ShapeDtypeStruct((2, B, N), F32)] * 3,
        in_specs=[vmem, vmem, vmem],
        out_specs=[vmem, vmem, vmem],
        scratch_shapes=scratch,
        compiler_params=pltpu.CompilerParams(
            collective_id=0, has_side_effects=True, vmem_limit_bytes=32 * 2**20),
        cost_estimate=pl.CostEstimate(flops=16 * 10**9, bytes_accessed=2 * 2**20, transcendentals=0),
        name="reduce_two_levels",
    )(coupling, potential, gain)
    return (kept - y)[None], (-minus_z)[None]


def solution(mesh):
    return jax.shard_map(
        local,
        mesh=mesh,
        in_specs=(P(), P("slab", None), P("slab", None)),
        out_specs=(P("slab", None, ("row", "col"), None), P("slab", None, ("row", "col"), None)),
        check_vma=False,
    )
```

time: 38 us -> 32 us (0.84)
  Pallas kernels: 33.2 us -> 28.5 us
  local copies, waits for them, and re-layouts: 3.9 us -> 1.22 us
  other arithmetic: 0 us -> 1.43 us
    pallas_call x1, Pallas kernels: 33.2 us -> 28.5 us  [local(): pl.pallas_call(kernel, out_shape=[jax.ShapeDtypeStruct((2, B, N), F32)] *...]
    unnamed x8 -> x4, local copies, waits for them, and re-layouts: 3.9 us -> 1.22 us
    broadcast_in_dim x0 -> x1, other arithmetic: none -> 0.73 us  [local(): return ((kept - y)[None], (-minus_z)[None])]
    mul x0 -> x2, other arithmetic: none -> 0.7 us  [the longest x1 0.7 us: local(): potential = disorder_width * (disorder.astype(F32) / 1023.0 - 0.5)]
where the time goes in v1:
time: 32 us; the launch traced here: 31.8 us
  Pallas kernels  28.5 us (89%)
  other arithmetic  1.43 us (4%)
  local copies, waits for them, and re-layouts  1.22 us (4%)
  between operations  0.66 us (2%)
    pallas_call x1, Pallas kernels, local(): pl.pallas_call(kernel, out_shape=[jax.ShapeDtypeStruct((2, B, N), F32)] *...  28.5 us
    unnamed x4, local copies, waits for them, and re-layouts  1.22 us
    broadcast_in_dim x1, other arithmetic, local(): return ((kept - y)[None], (-minus_z)[None])  0.73 us
    mul x1, other arithmetic, local(): potential = disorder_width * (disorder.astype(F32) / 1023.0 - 0.5)  0.7 us

profile of v1, /device:TPU:1, one launch (start us, length us, event | category | flops | bytes accessed | tf_op | source)
XLA Modules:
  0.0 31.8 jit_solution(6214739388108179572)
XLA Ops:
  0.6 0.0 copy-start.1
  0.6 0.7 %add_multiply_fusion.potential_ref = f32[2,512]{1,0:T(2,128)S(1)} fusion(s32[2,512]{1,0:T(2,128)} %param.4), kind=kLoop, calls=%fused_computation.3 | loop fusion | flops 4096 | bytes 8192 | tf_op jit(solution)/shard_map/mul | solution.py:273
  1.3 0.0 copy-done.1
  1.4 0.0 copy-start
  1.4 1.2 %copy-done = f32[512,512]{1,0:T(8,128)S(1)} copy-done((f32[512,512]{1,0:T(8,128)S(1)}, f32[512,512]{1,0:T(8,128)}, u32[]{:S(2)}) %copy-start) | copy-done | bytes 1048600
  2.6 28.5 %reduce_two_levels.1 = (f32[2,32,512]{2,1,0:T(8,128)S(1)}, f32[2,32,512]{2,1,0:T(8,128)S(1)}, f32[2,32,512]{2,1,0:T(8,128)S(1)}) custom-call(f32[512,512]{1,0:T(8,128)S(1)} %copy-done, f32[2,512]{1,0:T(2,128)S(1)} %add_multiply_fusion.potential_ref, f32[2,512]{1,0:T(2,128)S(1)} %convert_multiply_fusion.gain_ref), custom_call_target="tpu_custom_call" | custom-call | flops 16000000000 | bytes 2097152 | tf_op jit(solution)/shard_map/reduce_two_levels/pallas_call | solution.py:296
  31.1 0.7 %negate_bitcast_fusion = (f32[1,2,32,512]{3,2,1,0:T(8,128)}, f32[1,2,32,512]{3,2,1,0:T(8,128)}) fusion(f32[2,32,512]{2,1,0:T(8,128)S(1)} %get-tuple-element.7, f32[2,32,512]{2,1,0:T(8,128)S(1)} %get-tuple-element.5, f32[2,32,512]{2,1,0:T(8,128)S(1)} %get-tuple-element.6), kind=kLoop, calls=%fused_computation | loop fusion | flops 65536 | bytes 655360 | tf_op jit(solution)/shard_map/broadcast_in_dim | solution.py:307
  (1 shorter events, 0.0 us)
Async XLA Ops:
  0.6 0.7 %copy-start.1 = (s32[2,512]{1,0:T(2,128)S(1)}, s32[2,512]{1,0:T(2,128)}, u32[]{:S(2)}) copy-start(s32[2,512]{1,0:T(2,128)} %param.5) | copy-start | bytes 12292
  1.4 1.2 %copy-start = (f32[512,512]{1,0:T(8,128)S(1)}, f32[512,512]{1,0:T(8,128)}, u32[]{:S(2)}) copy-start(f32[512,512]{1,0:T(8,128)} %coupling_ref.1) | copy-start | bytes 3145732

commit v2 on v1

--- a/solution.py
+++ b/solution.py
@@ -40,7 +40,7 @@
     return a_re * b_re - a_im * b_im, a_re * b_im + a_im * b_re
 
 
-def kernel(coupling_ref, potential_ref, gain_ref, kept_ref, y_ref, minus_z_ref,
+def kernel(minus_k_ref, disorder_ref, gain_ref, kept_ref, y_ref, minus_z_ref,
            kf, kh, kl, a_buf, a_cols, w, q, qh, ql, m, mh, ml, lh, ll,
            acc, base, lband, f_send, z_send, s_send, f_recv, z_recv, s_recv,
            a_sems, f_sems, z_sems, s_sems):
@@ -77,10 +77,9 @@
             [jnp.sum(jnp.where(eye, ref[t * T:(t + 1) * T, t * T:(t + 1) * T], 0.0), axis=0, keepdims=True)
              for t in range(N // T)], axis=1)
 
-    potential = potential_ref[...]
-    gain = gain_ref[...]
-    k_diag = diagonal_of(coupling_ref)
-    d_re = (energy_level - potential) - k_diag
+    potential = disorder_width * (disorder_ref[...].astype(F32) / 1023.0 - 0.5)
+    gain = gain_step * gain_ref[...].astype(F32)
+    d_re = (energy_level - potential) + diagonal_of(minus_k_ref)
     d_im = absorption - gain
     size = d_re[1:2] * d_re[1:2] + d_im[1:2] * d_im[1:2]
     a_buf[1, 0:1, :] = d_re[1:2] / size
@@ -89,7 +88,7 @@
     for t in range(N // T):
         rows = slice(t * T, (t + 1) * T)
         ids = lax.broadcasted_iota(jnp.int32, (T, N), 0) + t * T
-        off = jnp.where(ids == lax.broadcasted_iota(jnp.int32, (T, N), 1), 0.0, coupling_ref[rows, :])
+        off = jnp.where(ids == lax.broadcasted_iota(jnp.int32, (T, N), 1), 0.0, -minus_k_ref[rows, :])
         kf[rows, :] = off
         hi, lo = split(off)
         kh[rows, :] = hi
@@ -212,12 +211,14 @@
         u = (u[:2 * half] + u[2 * half:]) + dot(hi, lo_ref[1])
         return t[:half] - u[half:], t[half:] + u[:half]
 
-    def inverse_step(index, carry):
-        re, im = times(*by_complex(acc[...], lh, ll), i_re, i_im)
-        acc[:W2, :] = base[:W2, :] - re
-        acc[W2:, :] = base[W2:, :] - im
+    def inverse_steps(index, carry):
+        rows = acc[...]
+        for repeat in range(2):
+            re, im = times(*by_complex(rows, lh, ll), i_re, i_im)
+            rows = base[...] - jnp.concatenate([re, im], axis=0)
+        acc[...] = rows
         return carry
-    lax.fori_loop(0, DEGREE, inverse_step, 0)
+    lax.fori_loop(0, DEGREE // 2, inverse_steps, 0)
 
     for part in range(2):
         f_send[part * B:(part + 1) * B, :] = acc[part * W2:part * W2 + B, :]
@@ -270,8 +271,7 @@
     square = (N, N)
     band = pltpu.VMEM((2, B, N), F32)
     rows = pltpu.VMEM((2 * B, N), F32)
-    potential = disorder_width * (disorder.astype(F32) / 1023.0 - 0.5)
-    gain = gain_step * gain_level.astype(F32)
+    minus_k, disorder, gain_level = (-coupling, disorder, gain_level)
     pair = pltpu.SemaphoreType.DMA((2,))
     scratch = [
         pltpu.VMEM(square, F32),
@@ -303,7 +303,7 @@
             collective_id=0, has_side_effects=True, vmem_limit_bytes=32 * 2**20),
         cost_estimate=pl.CostEstimate(flops=16 * 10**9, bytes_accessed=2 * 2**20, transcendentals=0),
         name="reduce_two_levels",
-    )(coupling, potential, gain)
+    )(minus_k, disorder, gain_level)
     return (kept - y)[None], (-minus_z)[None]
 
 

time: 32 us -> 31.4 us (0.981)
  local copies, waits for them, and re-layouts: 1.22 us -> 0.01 us
  other arithmetic: 1.43 us -> 2.05 us
    neg x0 -> x1, other arithmetic: none -> 1.33 us  [local(): minus_k, disorder, gain_level = (-coupling, disorder, gain_level)]
    unnamed x4, local copies, waits for them, and re-layouts: 1.22 us -> 0.01 us
    mul x2 -> x0, other arithmetic: 0.7 us -> none  [the longest x1 0.7 us: local(): potential = disorder_width * (disorder.astype(F32) / 1023.0 - 0.5)]
where the time goes in v2:
time: 31.4 us; the launch traced here: 31.2 us
  Pallas kernels  28.5 us (91%)
  other arithmetic  2.05 us (7%)
  between operations  0.68 us (2%)
    pallas_call x1, Pallas kernels, local(): pl.pallas_call(kernel, out_shape=[jax.ShapeDtypeStruct((2, B, N), F32)] *...  28.5 us
    neg x1, other arithmetic, local(): minus_k, disorder, gain_level = (-coupling, disorder, gain_level)  1.33 us
    broadcast_in_dim x1, other arithmetic, local(): return ((kept - y)[None], (-minus_z)[None])  0.73 us

profile of v2, /device:TPU:1, one launch (start us, length us, event | category | flops | bytes accessed | tf_op | source)
XLA Modules:
  0.0 31.2 jit_solution(7944053951821124597)
XLA Ops:
  0.6 0.0 copy-start.1
  0.6 0.0 copy-start
  0.6 1.3 %neg.6.minus_k_ref = f32[512,512]{1,0:T(8,128)S(1)} negate(f32[512,512]{1,0:T(8,128)} %param.3) | non-fusion elementwise | flops 262144 | bytes 2097152 | tf_op jit(solution)/shard_map/neg | solution.py:274
  2.0 0.0 copy-done.1
  2.0 0.0 copy-done
  2.0 28.5 %reduce_two_levels.1 = (f32[2,32,512]{2,1,0:T(8,128)S(1)}, f32[2,32,512]{2,1,0:T(8,128)S(1)}, f32[2,32,512]{2,1,0:T(8,128)S(1)}) custom-call(f32[512,512]{1,0:T(8,128)S(1)} %neg.6.minus_k_ref, s32[2,512]{1,0:T(2,128)S(1)} %copy-done, s32[2,512]{1,0:T(2,128)S(1)} %copy-done.1), custom_call_target="tpu_custom_call" | custom-call | flops 16000000000 | bytes 2097152 | tf_op jit(solution)/shard_map/reduce_two_levels/pallas_call | solution.py:296
  30.5 0.7 %negate_bitcast_fusion = (f32[1,2,32,512]{3,2,1,0:T(8,128)}, f32[1,2,32,512]{3,2,1,0:T(8,128)}) fusion(f32[2,32,512]{2,1,0:T(8,128)S(1)} %get-tuple-element.7, f32[2,32,512]{2,1,0:T(8,128)S(1)} %get-tuple-element.5, f32[2,32,512]{2,1,0:T(8,128)S(1)} %get-tuple-element.6), kind=kLoop, calls=%fused_computation | loop fusion | flops 65536 | bytes 655360 | tf_op jit(solution)/shard_map/broadcast_in_dim | solution.py:307
Async XLA Ops:
  0.6 1.4 %copy-start.1 = (s32[2,512]{1,0:T(2,128)S(1)}, s32[2,512]{1,0:T(2,128)}, u32[]{:S(2)}) copy-start(s32[2,512]{1,0:T(2,128)} %gain_ref.1) | copy-start | bytes 12292
  0.6 1.4 %copy-start = (s32[2,512]{1,0:T(2,128)S(1)}, s32[2,512]{1,0:T(2,128)}, u32[]{:S(2)}) copy-start(s32[2,512]{1,0:T(2,128)} %disorder_ref.1) | copy-start | bytes 12292
